TPU v7x, 32 devices: a whole 2x2x4 slice. The times are simulated.
32 devices in a mesh: tm: 8 (over z, core), space: 4 (over y, x).
Axes of the slice: x: 2, y: 2, z: 4, core: 2. Of those that a mesh axis runs over, the one named last changes fastest.
Arguments:
- starts: float32 [8, 48, 64, 128], P('tm', 'space'), may hold values from -45 to 45
- vel_x: float32 [48, 64, 128], P('space'), may hold values from -0.15 to 0.15
- vel_y: float32 [48, 64, 128], P('space'), may hold values from -0.15 to 0.15
- vel_z: float32 [48, 64, 128], P('space'), may hold values from -0.5 to 0.5
- kappa: float32 [48, 64, 128], P('space'), may hold values from 0.01 to 0.03
Outputs:
- new_starts: float32 [8, 48, 64, 128], P('tm', 'space')
- change_norm: float32 [], replicated
All inputs are finite; a program needn't handle non-finite values.
Results may differ from a plain program's by a relative error of at most 0.0003.
Values sent between devices are 32-bit elements; how exact they have to be, the bound alone decides.
A program may use at most 128 MiB of HBM per device.

v0:
```python
import jax
import jax.numpy as jnp
from jax import lax
from jax.sharding import PartitionSpec as P

FSTEPS = 6
GC = 2


def padded_2(value, sides, width):
    for axis, dim in sides:
        size, length = (lax.axis_size(axis), value.shape[dim])
        up = [(i, (i + 1) % size) for i in range(size - 1)]
        down = [(j, i) for i, j in up]
        last = lax.slice_in_dim(value, length - width, length, axis=dim)
        first = lax.slice_in_dim(value, 0, width, axis=dim)
        before = lax.ppermute(last, axis, up)
        after = lax.ppermute(first, axis, down)
        value = jnp.concatenate([before, value, after], axis=dim)
    return value


def from_behind(value, axis, steps):
    count = lax.axis_size(axis)
    first, last = (max(0, -steps), min(count, count - steps))
    return lax.ppermute(value, axis, [(source, source + steps) for source in range(first, last)])


def advance(extended, vel_x, vel_y, vel_z, kappa):
    padded = jnp.pad(extended, ((0, 0), (1, 1), (1, 1)))
    center = padded[1:-1, 1:-1, 1:-1]
    z_minus = padded[:-2, 1:-1, 1:-1]
    z_plus = padded[2:, 1:-1, 1:-1]
    y_minus = padded[1:-1, :-2, 1:-1]
    y_plus = padded[1:-1, 2:, 1:-1]
    x_minus = padded[1:-1, 1:-1, :-2]
    x_plus = padded[1:-1, 1:-1, 2:]
    transport = jnp.maximum(vel_x, 0.0) * (center - x_minus) + jnp.minimum(vel_x, 0.0) * (
        x_plus - center
    )
    transport = transport + (
        jnp.maximum(vel_y, 0.0) * (center - y_minus) + jnp.minimum(vel_y, 0.0) * (y_plus - center)
    )
    transport = transport + (
        jnp.maximum(vel_z, 0.0) * (center - z_minus) + jnp.minimum(vel_z, 0.0) * (z_plus - center)
    )
    diffusion = kappa * (x_minus + x_plus + y_minus + y_plus + z_minus + z_plus - 6.0 * center)
    return center - transport + diffusion


def zpad(field):
    return jnp.pad(field, ((1, 1), (0, 0), (0, 0)))


def restrict(field):
    depth, rows, cols = field.shape
    return field.reshape(depth // 4, 4, rows // 4, 4, cols // 4, 4).mean(axis=(1, 3, 5))


def prolong(field):
    depth, rows, cols = field.shape
    wide = jnp.broadcast_to(field[:, None, :, None, :, None], (depth, 4, rows, 4, cols, 4))
    return wide.reshape(depth * 4, rows * 4, cols * 4)


def per_device(starts, vel_x, vel_y, vel_z, kappa):
    start_state = starts[0]
    field = start_state
    for step_index in range(FSTEPS):
        extended = padded_2(field, (("space", 0),), 1)
        field = advance(extended, vel_x, vel_y, vel_z, kappa)
    courant_scale = FSTEPS / (4.0 * GC)
    diffusion_scale = FSTEPS / (16.0 * GC)
    coarse_set = jnp.stack(
        [
            restrict(start_state),
            restrict(field),
            restrict(vel_x) * courant_scale,
            restrict(vel_y) * courant_scale,
            restrict(vel_z) * courant_scale,
            restrict(kappa) * diffusion_scale,
        ]
    )
    coarse_depth = coarse_set.shape[1]
    coarse_set = lax.all_gather(coarse_set, "space", axis=1, tiled=True)

    def borders(coarse_field):
        return zpad(coarse_field)

    coarse_start = coarse_set[0]
    fine_coarse = coarse_set[1]

    def coarse(coarse_field):
        for step_index in range(GC):
            coarse_field = advance(
                borders(coarse_field), coarse_set[2], coarse_set[3], coarse_set[4], coarse_set[5]
            )
        return coarse_field

    drift_term = fine_coarse - coarse(coarse_start)
    slice_index = lax.axis_index("tm")
    chain_turns = lax.axis_size("tm") - 1

    def sweep_turn(turn_index, coarse_now):
        received = from_behind(coarse(coarse_now) + drift_term, "tm", 1)
        return jnp.where(slice_index == 0, coarse_start, received)

    current = lax.fori_loop(0, chain_turns, sweep_turn, coarse_start)
    current = lax.dynamic_slice_in_dim(
        current, lax.axis_index("space") * coarse_depth, coarse_depth, 0
    )
    received_end = from_behind(field, "tm", 1)
    corrected = received_end + prolong(current - restrict(received_end))
    new_state = jnp.where(slice_index == 0, start_state, corrected)
    local_sum = jnp.sum((new_state - start_state) ** 2)
    total_sum = lax.psum(local_sum, ("tm", "space"))
    cell_count = lax.axis_size("tm") * lax.axis_size("space") * new_state.size
    change = jnp.sqrt(total_sum / cell_count + 1e-06)
    return (new_state[None], change)


def solution(mesh):
    return jax.shard_map(
        per_device,
        mesh=mesh,
        in_specs=(
            P("tm", "space", None, None),
            P("space", None, None),
            P("space", None, None),
            P("space", None, None),
            P("space", None, None),
        ),
        out_specs=(P("tm", "space", None, None), P()),
        check_vma=False,
    )
```

profile of v0, /device:TPU:0, one launch (start us, length us, event | category | flops | bytes accessed | tf_op | source)
XLA Modules:
  0.0 327.1 jit_solution(9433766492707608201)
XLA Ops:
  1.6 4.8 %collective-permute-start.1 = (f32[1,64,128]{2,1,0:T(8,128)S(1)}, f32[1,64,128]{2,1,0:T(8,128)S(1)}, u32[]{:S(2)}, u32[]{:S(2)}) collective-permute-start(f32[1,64,128]{2,1,0:T(8,128)S(1)} %get-tuple-element.106), channel_id=1, source_target_pairs={{0,1},{1,2},{2,3},{4,5},{5,6},{6,7},{8,9},{9,10},{10,11},{12,13},{... | collective-permute-start | bytes 98312 | tf_op jit(solution)/shard_map/ppermute | solution.py:17
  8.0 4.2 %collective-permute-done.2 = f32[1,64,128]{2,1,0:T(8,128)S(1)} collective-permute-done((f32[1,64,128]{2,1,0:T(8,128)S(1)}, f32[1,64,128]{2,1,0:T(8,128)S(1)}, u32[]{:S(2)}, u32[]{:S(2)}) %collective-permute-start.2) | collective-permute-done | bytes 32800 | tf_op jit(solution)/shard_map/ppermute | solution.py:18
  16.1 4.3 %collective-permute-start.3 = (f32[1,64,128]{2,1,0:T(8,128)S(1)}, f32[1,64,128]{2,1,0:T(8,128)S(1)}, u32[]{:S(2)}, u32[]{:S(2)}) collective-permute-start(f32[1,64,128]{2,1,0:T(8,128)S(1)} %get-tuple-element.104), channel_id=1, source_target_pairs={{0,1},{1,2},{2,3},{4,5},{5,6},{6,7},{8,9},{9,10},{10,11},{12,13},{... | collective-permute-start | bytes 98312 | tf_op jit(solution)/shard_map/ppermute | solution.py:17
  22.0 4.2 %collective-permute-done.4 = f32[1,64,128]{2,1,0:T(8,128)S(1)} collective-permute-done((f32[1,64,128]{2,1,0:T(8,128)S(1)}, f32[1,64,128]{2,1,0:T(8,128)S(1)}, u32[]{:S(2)}, u32[]{:S(2)}) %collective-permute-start.4) | collective-permute-done | bytes 32800 | tf_op jit(solution)/shard_map/ppermute | solution.py:18
  43.5 4.5 %collective-permute-done.8 = f32[1,64,128]{2,1,0:T(8,128)S(1)} collective-permute-done((f32[1,64,128]{2,1,0:T(8,128)S(1)}, f32[1,64,128]{2,1,0:T(8,128)S(1)}, u32[]{:S(2)}, u32[]{:S(2)}) %collective-permute-start.8) | collective-permute-done | bytes 32800 | tf_op jit(solution)/shard_map/ppermute | solution.py:18
  50.3 4.5 %collective-permute-start.9 = (f32[1,64,128]{2,1,0:T(8,128)S(1)}, f32[1,64,128]{2,1,0:T(8,128)S(1)}, u32[]{:S(2)}, u32[]{:S(2)}) collective-permute-start(f32[1,64,128]{2,1,0:T(8,128)S(1)} %get-tuple-element.98), channel_id=1, source_target_pairs={{0,1},{1,2},{2,3},{4,5},{5,6},{6,7},{8,9},{9,10},{10,11},{12,13},{... | collective-permute-start | bytes 98312 | tf_op jit(solution)/shard_map/ppermute | solution.py:17
  54.9 14.3 %reshape_squeeze.3 = f32[3,4,16,4,32,4]{5,4,3,2,1,0:T(8,128)} reshape(f32[1,12,64,128]{3,2,1,0:T(8,128)S(1)} %copy-done.4) | data formatting | bytes 786432 | tf_op jit(solution)/shard_map/reshape;squeeze | solution.py:57
  69.2 5.6 %reduce_sum.72 = f32[3,16,32]{2,1,0:T(8,128)S(1)} reduce(f32[3,4,16,4,32,4]{5,4,3,2,1,0:T(8,128)} %reshape_squeeze.3, f32[]{:T(128)} %constant.59.clone.1), dimensions={1,3,5}, to_apply=%region_0.1 | reduce | flops 96768 | bytes 399364 | tf_op jit(solution)/shard_map/reduce_sum | solution.py:57
  80.7 14.3 %reshape.107 = f32[3,4,16,4,32,4]{5,4,3,2,1,0:T(8,128)} reshape(f32[12,64,128]{2,1,0:T(8,128)S(1)} %copy-done.3) | data formatting | bytes 786432 | tf_op jit(solution)/shard_map/reshape | solution.py:57
  95.0 14.3 %reshape.108 = f32[3,4,16,4,32,4]{5,4,3,2,1,0:T(8,128)} reshape(f32[12,64,128]{2,1,0:T(8,128)S(1)} %copy-done.2) | data formatting | bytes 786432 | tf_op jit(solution)/shard_map/reshape | solution.py:57
  109.3 14.3 %reshape.109 = f32[3,4,16,4,32,4]{5,4,3,2,1,0:T(8,128)} reshape(f32[12,64,128]{2,1,0:T(8,128)S(1)} %copy-done.1) | data formatting | bytes 786432 | tf_op jit(solution)/shard_map/reshape | solution.py:57
  123.7 14.3 %reshape.110 = f32[3,4,16,4,32,4]{5,4,3,2,1,0:T(8,128)} reshape(f32[12,64,128]{2,1,0:T(8,128)S(1)} %copy-done) | data formatting | bytes 786432 | tf_op jit(solution)/shard_map/reshape | solution.py:57
  138.0 5.6 %reduce_sum.74 = f32[3,16,32]{2,1,0:T(8,128)S(1)} reduce(f32[3,4,16,4,32,4]{5,4,3,2,1,0:T(8,128)} %reshape.107, f32[]{:T(128)} %constant.59.clone.1), dimensions={1,3,5}, to_apply=%region_2.3 | reduce | flops 96768 | bytes 399364 | tf_op jit(solution)/shard_map/reduce_sum | solution.py:57
  143.6 5.6 %reduce_sum.75 = f32[3,16,32]{2,1,0:T(8,128)S(1)} reduce(f32[3,4,16,4,32,4]{5,4,3,2,1,0:T(8,128)} %reshape.108, f32[]{:T(128)} %constant.59.clone.1), dimensions={1,3,5}, to_apply=%region_3.4 | reduce | flops 96768 | bytes 399364 | tf_op jit(solution)/shard_map/reduce_sum | solution.py:57
  149.1 5.6 %reduce_sum.76 = f32[3,16,32]{2,1,0:T(8,128)S(1)} reduce(f32[3,4,16,4,32,4]{5,4,3,2,1,0:T(8,128)} %reshape.109, f32[]{:T(128)} %constant.59.clone.1), dimensions={1,3,5}, to_apply=%region_4.5 | reduce | flops 96768 | bytes 399364 | tf_op jit(solution)/shard_map/reduce_sum | solution.py:57
  154.7 5.6 %reduce_sum.77 = f32[3,16,32]{2,1,0:T(8,128)S(1)} reduce(f32[3,4,16,4,32,4]{5,4,3,2,1,0:T(8,128)} %reshape.110, f32[]{:T(128)} %constant.59.clone.1), dimensions={1,3,5}, to_apply=%region_5.6 | reduce | flops 96768 | bytes 399364 | tf_op jit(solution)/shard_map/reduce_sum | solution.py:57
  161.3 14.3 %reshape.106 = f32[3,4,16,4,32,4]{5,4,3,2,1,0:T(8,128)} reshape(f32[12,64,128]{2,1,0:T(8,128)S(1)} %fusion.22) | data formatting | bytes 786432 | tf_op jit(solution)/shard_map/reshape | solution.py:57
  175.6 5.6 %reduce_sum.73 = f32[3,16,32]{2,1,0:T(8,128)S(1)} reduce(f32[3,4,16,4,32,4]{5,4,3,2,1,0:T(8,128)} %reshape.106, f32[]{:T(128)} %constant.59.clone.1), dimensions={1,3,5}, to_apply=%region_1.2 | reduce | flops 96768 | bytes 399364 | tf_op jit(solution)/shard_map/reduce_sum | solution.py:57
  181.2 11.7 %all_gather.3 = f32[6,12,16,32]{3,2,1,0:T(8,128)S(1)} all-gather(f32[6,3,16,32]{3,2,1,0:T(8,128)S(1)} %bitcast_dynamic-update-slice_fusion), channel_id=1, replica_groups=mesh['tm'=8,'space'=4] {'space'}, dimensions={1}, use_global_device_ids=true | all-gather | bytes 184320 | tf_op jit(solution)/shard_map/all_gather | solution.py:85
  195.6 14.3 %reshape.111 = f32[3,4,16,4,32,4]{5,4,3,2,1,0:T(8,128)} reshape(f32[12,64,128]{2,1,0:T(8,128)S(1)} %collective-permute-done.13) | data formatting | bytes 786432 | tf_op jit(solution)/shard_map/reshape | solution.py:57
  209.8 5.6 %reduce_sum.78 = f32[3,16,32]{2,1,0:T(8,128)S(1)} reduce(f32[3,4,16,4,32,4]{5,4,3,2,1,0:T(8,128)} %reshape.111, f32[]{:T(128)} %constant.59.clone.1), dimensions={1,3,5}, to_apply=%region_8.9 | reduce | flops 96768 | bytes 399364 | tf_op jit(solution)/shard_map/reduce_sum | solution.py:57
  215.4 47.1 %while.12 = (s32[]{:T(128)}, f32[12,16,32]{2,1,0:T(8,128)S(1)}, pred[]{:T(512)}, f32[6,12,16,32]{3,2,1,0:T(8,128)S(1)}, f32[12,16,32]{2,1,0:T(8,128)S(1)}, /*index=5*/f32[12,16,32]{2,1,0:T(8,128)S(1)}, s32[]{:T(128)}, f32[]{:T(128)}) while((s32[]{:T(128)}, f32[12,16,32]{2,1,0:T(8,128)S(1)}, pred[]{:T(512)}, f32[6,12,16,32]{3,2,1,0:T(8,128)S(1)}, ...), condition=%wide.region_7.8_spmd, body=%wide.region_6.7_spmd.sunk | while | flops 417794 | bytes 2031750 | solution.py:108
  215.8 7.6 %collective-permute-start = (f32[12,16,32]{2,1,0:T(8,128)S(1)}, f32[12,16,32]{2,1,0:T(8,128)S(1)}, u32[]{:S(2)}, u32[]{:S(2)}) collective-permute-start(f32[12,16,32]{2,1,0:T(8,128)S(1)} %fusion.114), channel_id=1, source_target_pairs={{0,4},{4,8},{8,12},{12,16},{16,20},{20,24},{24,28},{1,5},{5,9},{9,... | collective-permute-start | bytes 73736 | tf_op jit(solution)/shard_map/while/body/eval_jaxpr/ppermute | solution.py:26
  224.7 5.1 %collective-permute-start = (f32[12,16,32]{2,1,0:T(8,128)S(1)}, f32[12,16,32]{2,1,0:T(8,128)S(1)}, u32[]{:S(2)}, u32[]{:S(2)}) collective-permute-start(f32[12,16,32]{2,1,0:T(8,128)S(1)} %fusion.114), channel_id=1, source_target_pairs={{0,4},{4,8},{8,12},{12,16},{16,20},{20,24},{24,28},{1,5},{5,9},{9,... | collective-permute-start | bytes 73736 | tf_op jit(solution)/shard_map/while/body/eval_jaxpr/ppermute | solution.py:26
  231.2 5.0 %collective-permute-start = (f32[12,16,32]{2,1,0:T(8,128)S(1)}, f32[12,16,32]{2,1,0:T(8,128)S(1)}, u32[]{:S(2)}, u32[]{:S(2)}) collective-permute-start(f32[12,16,32]{2,1,0:T(8,128)S(1)} %fusion.114), channel_id=1, source_target_pairs={{0,4},{4,8},{8,12},{12,16},{16,20},{20,24},{24,28},{1,5},{5,9},{9,... | collective-permute-start | bytes 73736 | tf_op jit(solution)/shard_map/while/body/eval_jaxpr/ppermute | solution.py:26
  237.5 5.0 %collective-permute-start = (f32[12,16,32]{2,1,0:T(8,128)S(1)}, f32[12,16,32]{2,1,0:T(8,128)S(1)}, u32[]{:S(2)}, u32[]{:S(2)}) collective-permute-start(f32[12,16,32]{2,1,0:T(8,128)S(1)} %fusion.114), channel_id=1, source_target_pairs={{0,4},{4,8},{8,12},{12,16},{16,20},{20,24},{24,28},{1,5},{5,9},{9,... | collective-permute-start | bytes 73736 | tf_op jit(solution)/shard_map/while/body/eval_jaxpr/ppermute | solution.py:26
  243.9 5.0 %collective-permute-start = (f32[12,16,32]{2,1,0:T(8,128)S(1)}, f32[12,16,32]{2,1,0:T(8,128)S(1)}, u32[]{:S(2)}, u32[]{:S(2)}) collective-permute-start(f32[12,16,32]{2,1,0:T(8,128)S(1)} %fusion.114), channel_id=1, source_target_pairs={{0,4},{4,8},{8,12},{12,16},{16,20},{20,24},{24,28},{1,5},{5,9},{9,... | collective-permute-start | bytes 73736 | tf_op jit(solution)/shard_map/while/body/eval_jaxpr/ppermute | solution.py:26
  250.2 5.0 %collective-permute-start = (f32[12,16,32]{2,1,0:T(8,128)S(1)}, f32[12,16,32]{2,1,0:T(8,128)S(1)}, u32[]{:S(2)}, u32[]{:S(2)}) collective-permute-start(f32[12,16,32]{2,1,0:T(8,128)S(1)} %fusion.114), channel_id=1, source_target_pairs={{0,4},{4,8},{8,12},{12,16},{16,20},{20,24},{24,28},{1,5},{5,9},{9,... | collective-permute-start | bytes 73736 | tf_op jit(solution)/shard_map/while/body/eval_jaxpr/ppermute | solution.py:26
  256.6 5.0 %collective-permute-start = (f32[12,16,32]{2,1,0:T(8,128)S(1)}, f32[12,16,32]{2,1,0:T(8,128)S(1)}, u32[]{:S(2)}, u32[]{:S(2)}) collective-permute-start(f32[12,16,32]{2,1,0:T(8,128)S(1)} %fusion.114), channel_id=1, source_target_pairs={{0,4},{4,8},{8,12},{12,16},{16,20},{20,24},{24,28},{1,5},{5,9},{9,... | collective-permute-start | bytes 73736 | tf_op jit(solution)/shard_map/while/body/eval_jaxpr/ppermute | solution.py:26
  262.5 6.2 %broadcast_in_dim.4 = f32[3,4,16,4,32,4]{5,4,3,2,1,0:T(8,128)} broadcast(f32[3,16,32]{2,1,0:T(8,128)S(1)} %multiply_subtract_fusion), dimensions={0,2,4} | broadcast | bytes 399360 | tf_op jit(solution)/shard_map/broadcast_in_dim | solution.py:62
  268.8 11.5 %reshape.112 = f32[12,64,128]{2,1,0:T(8,128)S(1)} reshape(f32[3,4,16,4,32,4]{5,4,3,2,1,0:T(8,128)} %broadcast_in_dim.4) | data formatting | bytes 786432 | tf_op jit(solution)/shard_map/reshape | solution.py:63
  281.7 43.6 %psum.7 = f32[]{:T(128)} all-reduce(f32[]{:T(128)} %get-tuple-element.94), channel_id=1, replica_groups=mesh['tm'=8,'space'=4] {'tm','space'}, use_global_device_ids=true, to_apply=%region_10.11 | all-reduce | flops 1 | bytes 8 | tf_op jit(solution)/shard_map/psum | solution.py:116
  (104 shorter events, 47.4 us)
Async XLA Ops:
  0.6 54.2 %copy-start.4 = (f32[1,12,64,128]{3,2,1,0:T(8,128)S(1)}, f32[1,12,64,128]{3,2,1,0:T(8,128)}, u32[]{:S(2)}) copy-start(f32[1,12,64,128]{3,2,1,0:T(8,128)} %param.7) | copy-start | bytes 1179652
  0.6 37.5 %copy-start.1 = (f32[12,64,128]{2,1,0:T(8,128)S(1)}, f32[12,64,128]{2,1,0:T(8,128)}, u32[]{:S(2)}) copy-start(f32[12,64,128]{2,1,0:T(8,128)} %param.10) | copy-start | bytes 1179652
  0.7 37.5 %copy-start = (f32[12,64,128]{2,1,0:T(8,128)S(1)}, f32[12,64,128]{2,1,0:T(8,128)}, u32[]{:S(2)}) copy-start(f32[12,64,128]{2,1,0:T(8,128)} %param.11) | copy-start | bytes 1179652
  0.7 37.5 %copy-start.3 = (f32[12,64,128]{2,1,0:T(8,128)S(1)}, f32[12,64,128]{2,1,0:T(8,128)}, u32[]{:S(2)}) copy-start(f32[12,64,128]{2,1,0:T(8,128)} %param.8) | copy-start | bytes 1179652
  0.7 37.5 %copy-start.2 = (f32[12,64,128]{2,1,0:T(8,128)S(1)}, f32[12,64,128]{2,1,0:T(8,128)}, u32[]{:S(2)}) copy-start(f32[12,64,128]{2,1,0:T(8,128)} %param.9) | copy-start | bytes 1179652
  1.6 6.4 %collective-permute-start.1 = (f32[1,64,128]{2,1,0:T(8,128)S(1)}, f32[1,64,128]{2,1,0:T(8,128)S(1)}, u32[]{:S(2)}, u32[]{:S(2)}) collective-permute-start(f32[1,64,128]{2,1,0:T(8,128)S(1)} %get-tuple-element.106), channel_id=1, source_target_pairs={{0,1},{1,2},{2,3},{4,5},{5,6},{6,7},{8,9},{9,10},{10,11},{12,13},{... | collective-permute-start | bytes 98312 | tf_op jit(solution)/shard_map/ppermute | solution.py:17
  6.4 5.8 %collective-permute-start.2 = (f32[1,64,128]{2,1,0:T(8,128)S(1)}, f32[1,64,128]{2,1,0:T(8,128)S(1)}, u32[]{:S(2)}, u32[]{:S(2)}) collective-permute-start(f32[1,64,128]{2,1,0:T(8,128)S(1)} %get-tuple-element.107), channel_id=1, source_target_pairs={{1,0},{2,1},{3,2},{5,4},{6,5},{7,6},{9,8},{10,9},{11,10},{13,12},{... | collective-permute-start | bytes 98312 | tf_op jit(solution)/shard_map/ppermute | solution.py:18
  16.1 5.9 %collective-permute-start.3 = (f32[1,64,128]{2,1,0:T(8,128)S(1)}, f32[1,64,128]{2,1,0:T(8,128)S(1)}, u32[]{:S(2)}, u32[]{:S(2)}) collective-permute-start(f32[1,64,128]{2,1,0:T(8,128)S(1)} %get-tuple-element.104), channel_id=1, source_target_pairs={{0,1},{1,2},{2,3},{4,5},{5,6},{6,7},{8,9},{9,10},{10,11},{12,13},{... | collective-permute-start | bytes 98312 | tf_op jit(solution)/shard_map/ppermute | solution.py:17
  20.4 5.8 %collective-permute-start.4 = (f32[1,64,128]{2,1,0:T(8,128)S(1)}, f32[1,64,128]{2,1,0:T(8,128)S(1)}, u32[]{:S(2)}, u32[]{:S(2)}) collective-permute-start(f32[1,64,128]{2,1,0:T(8,128)S(1)} %get-tuple-element.105), channel_id=1, source_target_pairs={{1,0},{2,1},{3,2},{5,4},{6,5},{7,6},{9,8},{10,9},{11,10},{13,12},{... | collective-permute-start | bytes 98312 | tf_op jit(solution)/shard_map/ppermute | solution.py:18
  28.6 5.0 %collective-permute-start.5 = (f32[1,64,128]{2,1,0:T(8,128)S(1)}, f32[1,64,128]{2,1,0:T(8,128)S(1)}, u32[]{:S(2)}, u32[]{:S(2)}) collective-permute-start(f32[1,64,128]{2,1,0:T(8,128)S(1)} %get-tuple-element.102), channel_id=1, source_target_pairs={{0,1},{1,2},{2,3},{4,5},{5,6},{6,7},{8,9},{9,10},{10,11},{12,13},{... | collective-permute-start | bytes 98312 | tf_op jit(solution)/shard_map/ppermute | solution.py:17
  32.0 5.8 %collective-permute-start.6 = (f32[1,64,128]{2,1,0:T(8,128)S(1)}, f32[1,64,128]{2,1,0:T(8,128)S(1)}, u32[]{:S(2)}, u32[]{:S(2)}) collective-permute-start(f32[1,64,128]{2,1,0:T(8,128)S(1)} %get-tuple-element.103), channel_id=1, source_target_pairs={{1,0},{2,1},{3,2},{5,4},{6,5},{7,6},{9,8},{10,9},{11,10},{13,12},{... | collective-permute-start | bytes 98312 | tf_op jit(solution)/shard_map/ppermute | solution.py:18
  38.8 4.7 %collective-permute-start.7 = (f32[1,64,128]{2,1,0:T(8,128)S(1)}, f32[1,64,128]{2,1,0:T(8,128)S(1)}, u32[]{:S(2)}, u32[]{:S(2)}) collective-permute-start(f32[1,64,128]{2,1,0:T(8,128)S(1)} %get-tuple-element.100), channel_id=1, source_target_pairs={{0,1},{1,2},{2,3},{4,5},{5,6},{6,7},{8,9},{9,10},{10,11},{12,13},{... | collective-permute-start | bytes 98312 | tf_op jit(solution)/shard_map/ppermute | solution.py:17
  41.9 6.1 %collective-permute-start.8 = (f32[1,64,128]{2,1,0:T(8,128)S(1)}, f32[1,64,128]{2,1,0:T(8,128)S(1)}, u32[]{:S(2)}, u32[]{:S(2)}) collective-permute-start(f32[1,64,128]{2,1,0:T(8,128)S(1)} %get-tuple-element.101), channel_id=1, source_target_pairs={{1,0},{2,1},{3,2},{5,4},{6,5},{7,6},{9,8},{10,9},{11,10},{13,12},{... | collective-permute-start | bytes 98312 | tf_op jit(solution)/shard_map/ppermute | solution.py:18
  49.0 25.8 %collective-permute-start.10 = (f32[1,64,128]{2,1,0:T(8,128)S(1)}, f32[1,64,128]{2,1,0:T(8,128)S(1)}, u32[]{:S(2)}, u32[]{:S(2)}) collective-permute-start(f32[1,64,128]{2,1,0:T(8,128)S(1)} %get-tuple-element.99), channel_id=1, source_target_pairs={{1,0},{2,1},{3,2},{5,4},{6,5},{7,6},{9,8},{10,9},{11,10},{13,12},{... | collective-permute-start | bytes 98312 | tf_op jit(solution)/shard_map/ppermute | solution.py:18
  50.3 24.5 %collective-permute-start.9 = (f32[1,64,128]{2,1,0:T(8,128)S(1)}, f32[1,64,128]{2,1,0:T(8,128)S(1)}, u32[]{:S(2)}, u32[]{:S(2)}) collective-permute-start(f32[1,64,128]{2,1,0:T(8,128)S(1)} %get-tuple-element.98), channel_id=1, source_target_pairs={{0,1},{1,2},{2,3},{4,5},{5,6},{6,7},{8,9},{9,10},{10,11},{12,13},{... | collective-permute-start | bytes 98312 | tf_op jit(solution)/shard_map/ppermute | solution.py:17
  75.8 84.5 %collective-permute-start.11 = (f32[1,64,128]{2,1,0:T(8,128)S(1)}, f32[1,64,128]{2,1,0:T(8,128)S(1)}, u32[]{:S(2)}, u32[]{:S(2)}) collective-permute-start(f32[1,64,128]{2,1,0:T(8,128)S(1)} %get-tuple-element.96), channel_id=1, source_target_pairs={{0,1},{1,2},{2,3},{4,5},{5,6},{6,7},{8,9},{9,10},{10,11},{12,13},{... | collective-permute-start | bytes 98312 | tf_op jit(solution)/shard_map/ppermute | solution.py:17
  79.2 81.1 %collective-permute-start.12 = (f32[1,64,128]{2,1,0:T(8,128)S(1)}, f32[1,64,128]{2,1,0:T(8,128)S(1)}, u32[]{:S(2)}, u32[]{:S(2)}) collective-permute-start(f32[1,64,128]{2,1,0:T(8,128)S(1)} %get-tuple-element.97), channel_id=1, source_target_pairs={{1,0},{2,1},{3,2},{5,4},{6,5},{7,6},{9,8},{10,9},{11,10},{13,12},{... | collective-permute-start | bytes 98312 | tf_op jit(solution)/shard_map/ppermute | solution.py:18
  192.9 2.6 collective-permute-start.13
  215.8 8.5 %collective-permute-start = (f32[12,16,32]{2,1,0:T(8,128)S(1)}, f32[12,16,32]{2,1,0:T(8,128)S(1)}, u32[]{:S(2)}, u32[]{:S(2)}) collective-permute-start(f32[12,16,32]{2,1,0:T(8,128)S(1)} %fusion.114), channel_id=1, source_target_pairs={{0,4},{4,8},{8,12},{12,16},{16,20},{20,24},{24,28},{1,5},{5,9},{9,... | collective-permute-start | bytes 73736 | tf_op jit(solution)/shard_map/while/body/eval_jaxpr/ppermute | solution.py:26
  224.7 6.0 %collective-permute-start = (f32[12,16,32]{2,1,0:T(8,128)S(1)}, f32[12,16,32]{2,1,0:T(8,128)S(1)}, u32[]{:S(2)}, u32[]{:S(2)}) collective-permute-start(f32[12,16,32]{2,1,0:T(8,128)S(1)} %fusion.114), channel_id=1, source_target_pairs={{0,4},{4,8},{8,12},{12,16},{16,20},{20,24},{24,28},{1,5},{5,9},{9,... | collective-permute-start | bytes 73736 | tf_op jit(solution)/shard_map/while/body/eval_jaxpr/ppermute | solution.py:26
  231.2 5.9 %collective-permute-start = (f32[12,16,32]{2,1,0:T(8,128)S(1)}, f32[12,16,32]{2,1,0:T(8,128)S(1)}, u32[]{:S(2)}, u32[]{:S(2)}) collective-permute-start(f32[12,16,32]{2,1,0:T(8,128)S(1)} %fusion.114), channel_id=1, source_target_pairs={{0,4},{4,8},{8,12},{12,16},{16,20},{20,24},{24,28},{1,5},{5,9},{9,... | collective-permute-start | bytes 73736 | tf_op jit(solution)/shard_map/while/body/eval_jaxpr/ppermute | solution.py:26
  237.5 5.9 %collective-permute-start = (f32[12,16,32]{2,1,0:T(8,128)S(1)}, f32[12,16,32]{2,1,0:T(8,128)S(1)}, u32[]{:S(2)}, u32[]{:S(2)}) collective-permute-start(f32[12,16,32]{2,1,0:T(8,128)S(1)} %fusion.114), channel_id=1, source_target_pairs={{0,4},{4,8},{8,12},{12,16},{16,20},{20,24},{24,28},{1,5},{5,9},{9,... | collective-permute-start | bytes 73736 | tf_op jit(solution)/shard_map/while/body/eval_jaxpr/ppermute | solution.py:26
  243.9 5.9 %collective-permute-start = (f32[12,16,32]{2,1,0:T(8,128)S(1)}, f32[12,16,32]{2,1,0:T(8,128)S(1)}, u32[]{:S(2)}, u32[]{:S(2)}) collective-permute-start(f32[12,16,32]{2,1,0:T(8,128)S(1)} %fusion.114), channel_id=1, source_target_pairs={{0,4},{4,8},{8,12},{12,16},{16,20},{20,24},{24,28},{1,5},{5,9},{9,... | collective-permute-start | bytes 73736 | tf_op jit(solution)/shard_map/while/body/eval_jaxpr/ppermute | solution.py:26
  250.2 5.9 %collective-permute-start = (f32[12,16,32]{2,1,0:T(8,128)S(1)}, f32[12,16,32]{2,1,0:T(8,128)S(1)}, u32[]{:S(2)}, u32[]{:S(2)}) collective-permute-start(f32[12,16,32]{2,1,0:T(8,128)S(1)} %fusion.114), channel_id=1, source_target_pairs={{0,4},{4,8},{8,12},{12,16},{16,20},{20,24},{24,28},{1,5},{5,9},{9,... | collective-permute-start | bytes 73736 | tf_op jit(solution)/shard_map/while/body/eval_jaxpr/ppermute | solution.py:26
  256.6 5.9 %collective-permute-start = (f32[12,16,32]{2,1,0:T(8,128)S(1)}, f32[12,16,32]{2,1,0:T(8,128)S(1)}, u32[]{:S(2)}, u32[]{:S(2)}) collective-permute-start(f32[12,16,32]{2,1,0:T(8,128)S(1)} %fusion.114), channel_id=1, source_target_pairs={{0,4},{4,8},{8,12},{12,16},{16,20},{20,24},{24,28},{1,5},{5,9},{9,... | collective-permute-start | bytes 73736 | tf_op jit(solution)/shard_map/while/body/eval_jaxpr/ppermute | solution.py:26
where the time goes:
time: 328 us; the launch traced here: 327 us
  local copies, waits for them, and re-layouts  119 us (36%)
  starting transfers between devices  70.6 us (22%)
  blocking collectives  55.2 us (17%)
  other arithmetic  53.3 us (16%)
  waiting for transfers between devices  25.7 us (8%)
    reshape x6, local copies, waits for them, and re-layouts, restrict(): field.reshape(depth // 4, 4, rows // 4, 4, cols // 4, 4)  85.9 us
    psum x1, blocking collectives, per_device(): total_sum = lax.psum(local_sum, ('tm', 'space'))  43.6 us
    ppermute x8, starting transfers between devices, from_behind(): lax.ppermute(value, axis, [(source, source + steps) for source in range(f...  39 us
    reduce_sum x7, other arithmetic, restrict(): field.reshape(depth // 4, 4, rows // 4, 4, cols // 4, 4)  39 us
    ppermute x6, starting transfers between devices, padded_2(): before = lax.ppermute(last, axis, up)  23.7 us
    ppermute x6, waiting for transfers between devices, padded_2(): after = lax.ppermute(first, axis, down)  17.2 us
    another operation x1, local copies, waits for them, and re-layouts, restrict(): field.reshape(depth // 4, 4, rows // 4, 4, cols // 4, 4)  14.3 us
    all_gather x1, blocking collectives, per_device(): coarse_set = lax.all_gather(coarse_set, 'space', axis=1, tiled=True)  11.7 us
  transfers between devices with their start and end apart: 20, of which 16 were waited for; matrix products, arithmetic and copies ran while one was open for 31% of the time, Pallas kernels for 0%

commit v1 on v0

v1 whole, which is shorter than its diff:
```python
import functools

import jax
import jax.numpy as jnp
from jax import lax
from jax.experimental import pallas as pl
from jax.experimental.pallas import tpu as pltpu
from jax.sharding import PartitionSpec as P

FSTEPS = 6
GC = 2
B = 4
ROUNDS = (2, 2, 2)
HALO = max(ROUNDS)
MESH = pl.DeviceIdType.MESH


def dot(a, b):
    return jnp.dot(
        a, b, precision=lax.Precision.HIGHEST, preferred_element_type=jnp.float32
    )


def iota(shape, dim):
    return lax.broadcasted_iota(jnp.int32, shape, dim)


def group_mask(rows, lanes):
    group = (iota((rows, lanes), 0) // B) % B
    return group == iota((rows, lanes), 1) // (lanes // B)


def pool(sums, packed_rows):
    rows, lanes = sums.shape
    cols = lanes // B
    spread = iota((lanes, lanes), 0) // B == iota((lanes, lanes), 1) % cols
    wide = dot(sums, jnp.where(spread, 1.0 / B**3, 0.0).astype(jnp.float32))
    wide = jnp.where(group_mask(rows, lanes), wide, 0.0)
    pick = iota((packed_rows, rows), 1) // B**2 == iota((packed_rows, rows), 0)
    return dot(pick.astype(jnp.float32), wide)


def prolong(packed, rows, first):
    lanes = packed.shape[1]
    cols = lanes // B
    shape = (rows, packed.shape[0])
    pick = iota(shape, 0) // B**2 + first == iota(shape, 1)
    wide = dot(pick.astype(jnp.float32), packed)
    wide = jnp.where(group_mask(rows, lanes), wide, 0.0)
    spread = iota((lanes, lanes), 0) % cols == iota((lanes, lanes), 1) // B
    return dot(wide, spread.astype(jnp.float32))


def weights(vx, vy, vz, k, edges):
    low_x, high_x, low_y, high_y, low_z, high_z = edges

    def inside(edge, value):
        return value if edge is None else jnp.where(edge, 0.0, value)

    return (
        1.0 - jnp.abs(vx) - jnp.abs(vy) - jnp.abs(vz) - 6.0 * k,
        inside(low_x, k + jnp.maximum(vx, 0.0)),
        inside(high_x, k - jnp.minimum(vx, 0.0)),
        inside(low_y, k + jnp.maximum(vy, 0.0)),
        inside(high_y, k - jnp.minimum(vy, 0.0)),
        inside(low_z, k + jnp.maximum(vz, 0.0)),
        inside(high_z, k - jnp.minimum(vz, 0.0)),
    )


def kernel(
    T, S,
    st_hbm, vx_hbm, vy_hbm, vz_hbm, kp_hbm,
    out_ref, chg_ref,
    cx, co, U, V, st, F, wloc, wg, ccloc, ccg, qloc, qg, full, cfull, cw, hs,
    lsem, usend, urecv, csend, crecv, hsend, hrecv, ccsend, ccrecv,
    wsend, wrecv, qsend, qrecv,
):
    depth, Y, X = st.shape
    N = T * S
    t = lax.axis_index("tm")
    s = lax.axis_index("space")
    me = t * S + s
    planes = depth // B
    slab_rows = planes * Y // B**2
    plane_rows = Y // B**2
    pad_rows = wloc.shape[0]
    H = HALO
    coefs = (vx_hbm, vy_hbm, vz_hbm, kp_hbm)

    def peer(i):
        return lax.rem(t + i // S, T), lax.rem(s + lax.rem(i, S), S)

    loads = [
        pltpu.make_async_copy(c, cx.at[i, pl.ds(H - 1, depth)], lsem.at[i])
        for i, c in enumerate(coefs)
    ]
    load_st = pltpu.make_async_copy(st_hbm.at[0], st, lsem.at[4])
    for c in loads:
        c.start()
    load_st.start()

    barrier = pltpu.get_barrier_semaphore()

    def greet(i, _):
        pl.semaphore_signal(barrier, inc=1, device_id=peer(i), device_id_type=MESH)
        return 0

    lax.fori_loop(1, N, greet, 0)

    @pl.when(s == 0)
    def _():
        for r in range(len(ROUNDS)):
            U[r, 0:H] = jnp.zeros((H, Y, X), jnp.float32)
        if H > 1:
            cx[:, 0 : H - 1] = jnp.zeros((4, H - 1, Y, X), jnp.float32)

    @pl.when(s == S - 1)
    def _():
        for r in range(len(ROUNDS)):
            U[r, H + depth : 2 * H + depth] = jnp.zeros((H, Y, X), jnp.float32)
        if H > 1:
            cx[:, H - 1 + depth : 2 * H - 2 + depth] = jnp.zeros((4, H - 1, Y, X), jnp.float32)

    for c in loads:
        c.wait()
    load_st.wait()

    lane = iota((Y, X), 1)
    row = iota((Y, X), 0)
    edges = (lane == 0, lane == X - 1, row == 0, row == Y - 1, None, None)

    def fill(z, _):
        for i, w in enumerate(weights(cx[0, z], cx[1, z], cx[2, z], cx[3, z], edges)):
            co[i, z] = w
        return 0

    lax.fori_loop(H - 1, H - 1 + depth, fill, 0)

    for i in range(4):
        sums = [
            cx[i, H - 1 + B * p] + cx[i, H + B * p] + cx[i, H + 1 + B * p] + cx[i, H + 2 + B * p]
            for p in range(planes)
        ]
        ccloc[i] = pool(jnp.concatenate(sums, axis=0), pad_rows)
    ccg[pl.ds(s, 1)] = ccloc[...][None]

    pl.semaphore_wait(barrier, N - 1)

    def remote(src, dst, send, recv, device):
        return pltpu.make_async_remote_copy(
            src_ref=src, dst_ref=dst, send_sem=send, recv_sem=recv,
            device_id=device, device_id_type=MESH,
        )

    d0 = ROUNDS[0]
    up_t = lax.rem(t + 1, T)
    up_s = lax.rem(s + 1, S)
    down_s = lax.rem(s + S - 1, S)
    has_up = s < S - 1
    has_down = s > 0
    moves = t < T - 1
    works = t > 0
    low0 = remote(st_hbm.at[0, pl.ds(depth - d0, d0)], U.at[0, pl.ds(H - d0, d0)],
                  usend.at[0], urecv.at[0], (up_t, up_s))
    high0 = remote(st_hbm.at[0, pl.ds(0, d0)], U.at[0, pl.ds(H + depth, d0)],
                   usend.at[1], urecv.at[1], (up_t, down_s))
    main0 = remote(st_hbm.at[0], U.at[0, pl.ds(H, depth)],
                   usend.at[2], urecv.at[2], (up_t, s))
    low_c = [
        remote(c.at[pl.ds(depth - H + 1, H - 1)], cx.at[i, pl.ds(0, H - 1)],
               csend.at[0, i], crecv.at[0, i], (t, up_s))
        for i, c in enumerate(coefs)
    ] if H > 1 else []
    high_c = [
        remote(c.at[pl.ds(0, H - 1)], cx.at[i, pl.ds(H - 1 + depth, H - 1)],
               csend.at[1, i], crecv.at[1, i], (t, down_s))
        for i, c in enumerate(coefs)
    ] if H > 1 else []

    @pl.when(moves)
    def _():
        main0.start()

    @pl.when(moves & has_up)
    def _():
        low0.start()

    @pl.when(moves & has_down)
    def _():
        high0.start()

    @pl.when(works & has_up)
    def _():
        for c in low_c:
            c.start()

    @pl.when(works & has_down)
    def _():
        for c in high_c:
            c.start()

    def cc_copy(j, slot):
        return remote(ccloc, ccg.at[slot], ccsend.at[j], ccrecv.at[slot],
                      (t, lax.rem(s + j, S)))

    for j in range(1, S):
        cc_copy(j, s).start()

    def step(src, dst, lo, hi):
        def body(z, _):
            u = src[z]
            v = co[0, z - 1] * u
            v += co[1, z - 1] * pltpu.roll(u, 1, 1)
            v += co[2, z - 1] * pltpu.roll(u, X - 1, 1)
            v += co[3, z - 1] * pltpu.roll(u, 1, 0)
            v += co[4, z - 1] * pltpu.roll(u, Y - 1, 0)
            v += co[5, z - 1] * src[z - 1]
            v += co[6, z - 1] * src[z + 1]
            dst[z] = v
            return 0

        lax.fori_loop(lo, hi, body, 0)

    def w_copy(i, slot):
        return remote(wloc.at[pl.ds(0, slab_rows)], wg.at[slot, pl.ds(0, slab_rows)],
                      wsend.at[i], wrecv.at[slot], peer(i))

    def q_copy(i, slot):
        return remote(qloc, qg.at[slot], qsend.at[i], qrecv.at[slot], peer(i))

    @pl.when(works)
    def _():
        @pl.when(has_down)
        def _():
            for c in low_c:
                c.wait_recv()
            lax.fori_loop(0, H - 1, fill, 0)
            low0.wait_recv()

        @pl.when(has_up)
        def _():
            for c in high_c:
                c.wait_recv()
            lax.fori_loop(H - 1 + depth, 2 * H - 2 + depth, fill, 0)
            high0.wait_recv()

        @pl.when(s == 0)
        def _():
            lax.fori_loop(0, H - 1, fill, 0)

        @pl.when(s == S - 1)
        def _():
            lax.fori_loop(H - 1 + depth, 2 * H - 2 + depth, fill, 0)

        main0.wait_recv()

        for r, d in enumerate(ROUNDS):
            if r > 0:
                low = remote(U.at[r, pl.ds(H + depth - d, d)], U.at[r, pl.ds(H - d, d)],
                             hsend.at[r, 0], hrecv.at[r, 0], (t, up_s))
                high = remote(U.at[r, pl.ds(H, d)], U.at[r, pl.ds(H + depth, d)],
                              hsend.at[r, 1], hrecv.at[r, 1], (t, down_s))

                @pl.when(has_up)
                def _(low=low):
                    low.start()

                @pl.when(has_down)
                def _(high=high):
                    high.start()

                @pl.when(has_down)
                def _(low=low):
                    low.wait_recv()

                @pl.when(has_up)
                def _(high=high):
                    high.wait_recv()
            src = U.at[r]
            for j in range(1, d + 1):
                dst = U.at[r + 1] if j == d else V.at[j % 2]
                step(src, dst, H - d + j, H + depth + d - j)
                src = dst
            if r > 0:
                @pl.when(has_up)
                def _(low=low):
                    low.wait_send()

                @pl.when(has_down)
                def _(high=high):
                    high.wait_send()

        R = len(ROUNDS)
        sums = []
        for p in range(planes):
            total = None
            for z in range(B * p, B * p + B):
                f = U[R, H + z] - st[z]
                F[z] = f
                total = f if total is None else total + f
            sums.append(total)
        wloc[...] = pool(jnp.concatenate(sums, axis=0), pad_rows)

        def send_w(i, _):
            w_copy(i, me).start()
            return 0

        lax.fori_loop(1, N, send_w, 0)
        wg[pl.ds(me, 1)] = wloc[...][None]

        wide = prolong(wloc[...], planes * Y, 0)
        q = jnp.zeros((8, X), jnp.float32)
        for p in range(planes):
            mean = wide[p * Y : (p + 1) * Y]
            for z in range(B * p, B * p + B):
                g = F[z] - mean
                q += jnp.sum((g * g).reshape(Y // 8, 8, X), axis=0)
        qloc[...] = jnp.sum(q, axis=0, keepdims=True)

        def send_q(i, _):
            q_copy(i, me).start()
            return 0

        lax.fori_loop(1, N, send_q, 0)
        qg[pl.ds(me, 1)] = qloc[...][None]

    for j in range(1, S):
        cc_copy(j, lax.rem(s + S - j, S)).wait_recv()
    for p in range(S):
        cfull[:, p * slab_rows : (p + 1) * slab_rows] = ccg[p, :, 0:slab_rows]
    rows = S * slab_rows
    crow = iota((rows, X), 0)
    clane = iota((rows, X), 1)
    cols = X // B
    group = clane // cols
    y_high = lax.rem(crow, plane_rows)
    courant = FSTEPS / (4.0 * GC)
    spread = FSTEPS / (16.0 * GC)
    for i, w in enumerate(weights(
        cfull[0] * courant, cfull[1] * courant, cfull[2] * courant, cfull[3] * spread,
        (
            lax.rem(clane, cols) == 0,
            lax.rem(clane, cols) == cols - 1,
            (y_high == 0) & (group == 0),
            (y_high == plane_rows - 1) & (group == B - 1),
            crow < plane_rows,
            crow >= rows - plane_rows,
        ),
    )):
        cw[i] = w

    def coarse(u):
        for _ in range(GC):
            below = jnp.where(group == B - 1, pltpu.roll(u, 1, 0), u)
            above = jnp.where(group == 0, pltpu.roll(u, rows - 1, 0), u)
            v = cw[0] * u
            v += cw[1] * pltpu.roll(u, 1, 1)
            v += cw[2] * pltpu.roll(u, X - 1, 1)
            v += cw[3] * pltpu.roll(below, cols, 1)
            v += cw[4] * pltpu.roll(above, X - cols, 1)
            v += cw[5] * pltpu.roll(u, plane_rows, 0)
            v += cw[6] * pltpu.roll(u, rows - plane_rows, 0)
            u = v
        return u

    def arrival(copy, slot):
        @pl.when(slot != me)
        def _():
            copy(1, slot).wait_recv()

    def chain(m, carry):
        jump, squares = carry
        for p in range(S):
            arrival(w_copy, m * S + p)
        for p in range(S):
            full[p * slab_rows : (p + 1) * slab_rows] = wg[m * S + p, 0:slab_rows]
        moved = coarse(jump)
        hs[m] = moved
        jump = full[...] + moved
        return jump, squares + jump * jump

    zero = jnp.zeros((rows, X), jnp.float32)
    _, squares = lax.fori_loop(1, T, chain, (zero, zero))

    @pl.when(works)
    def _():
        wide = prolong(hs[t], planes * Y, s * slab_rows)
        for z in range(depth):
            p = z // B
            out_ref[0, z] = U[len(ROUNDS), H + z] + wide[p * Y : (p + 1) * Y]

    @pl.when(t == 0)
    def _():
        out_ref[0] = st[...]

    def gather_q(i, total):
        arrival(q_copy, i)
        return total + qg[i]

    total = lax.fori_loop(S, N, gather_q, jnp.zeros((1, X), jnp.float32))
    total = total + float(B**3) * jnp.sum(squares, axis=0, keepdims=True)
    total = jnp.sum(total, axis=1, keepdims=True)
    count = N * depth * Y * X
    chg_ref[...] = jnp.sqrt(total / count + 1e-6)

    for j in range(1, S):
        cc_copy(j, s).wait_send()

    @pl.when(moves)
    def _():
        main0.wait_send()

    @pl.when(moves & has_up)
    def _():
        low0.wait_send()

    @pl.when(moves & has_down)
    def _():
        high0.wait_send()

    @pl.when(works & has_up)
    def _():
        for c in low_c:
            c.wait_send()

    @pl.when(works & has_down)
    def _():
        for c in high_c:
            c.wait_send()

    @pl.when(works)
    def _():
        def done(i, _):
            w_copy(i, me).wait_send()
            q_copy(i, me).wait_send()
            return 0

        lax.fori_loop(1, N, done, 0)


def per_device(T, S, starts, vel_x, vel_y, vel_z, kappa):
    depth, Y, X = vel_x.shape
    slab_rows = depth // B * Y // B**2
    pad_rows = -(-slab_rows // 8) * 8
    rows = S * slab_rows
    N = T * S
    R = len(ROUNDS)
    vmem = lambda *shape: pltpu.VMEM(shape, jnp.float32)
    dma = lambda *shape: pltpu.SemaphoreType.DMA(shape)
    ext = depth + 2 * HALO
    new, change = pl.pallas_call(
        functools.partial(kernel, T, S),
        out_shape=(
            jax.ShapeDtypeStruct(starts.shape, jnp.float32),
            jax.ShapeDtypeStruct((1, 1), jnp.float32),
        ),
        in_specs=[pl.BlockSpec(memory_space=pl.ANY)] * 5,
        out_specs=(
            pl.BlockSpec(memory_space=pltpu.VMEM),
            pl.BlockSpec(memory_space=pltpu.VMEM),
        ),
        scratch_shapes=[
            vmem(4, ext - 2, Y, X),
            vmem(7, ext - 2, Y, X),
            vmem(R + 1, ext, Y, X),
            vmem(2, ext, Y, X),
            vmem(depth, Y, X),
            vmem(depth, Y, X),
            vmem(pad_rows, X),
            vmem(N, pad_rows, X),
            vmem(4, pad_rows, X),
            vmem(S, 4, pad_rows, X),
            vmem(1, X),
            vmem(N, 1, X),
            vmem(rows, X),
            vmem(4, rows, X),
            vmem(7, rows, X),
            vmem(T, rows, X),
            dma(5),
            dma(3), dma(3),
            dma(2, 4), dma(2, 4),
            dma(R, 2), dma(R, 2),
            dma(S), dma(S),
            dma(N), dma(N),
            dma(N), dma(N),
        ],
        compiler_params=pltpu.CompilerParams(
            collective_id=0, has_side_effects=True, vmem_limit_bytes=40 * 2**20
        ),
    )(starts, vel_x, vel_y, vel_z, kappa)
    return new, change[0, 0]


def solution(mesh):
    T, S = mesh.shape["tm"], mesh.shape["space"]
    return jax.shard_map(
        functools.partial(per_device, T, S),
        mesh=mesh,
        in_specs=(
            P("tm", "space", None, None),
            P("space", None, None),
            P("space", None, None),
            P("space", None, None),
            P("space", None, None),
        ),
        out_specs=(P("tm", "space", None, None), P()),
        check_vma=False,
    )
```

time: 328 us -> 54 us (0.16)
  local copies, waits for them, and re-layouts: 119 us -> 5.72 us
  starting transfers between devices: 70.6 us -> 0 us
  blocking collectives: 55.2 us -> 0 us
  other arithmetic: 53.3 us -> 0 us
  Pallas kernels: 0 us -> 44.9 us
  waiting for transfers between devices: 25.7 us -> 0 us
    reshape x7 -> x0, local copies, waits for them, and re-layouts: 97.4 us -> none  [the longest x6 85.9 us: restrict(): field.reshape(depth // 4, 4, rows // 4, 4, cols // 4, 4)]
    ppermute x20 -> x0, starting transfers between devices: 70.6 us -> none  [the longest x8 39 us: from_behind(): lax.ppermute(value, axis, [(source, source + steps) for source in range(f...]
    pallas_call x0 -> x1, Pallas kernels: none -> 44.9 us  [per_device(): pl.pallas_call(functools.partial(kernel, T, S), out_shape=(jax.ShapeDtype...]
    psum x1 -> x0, blocking collectives: 43.6 us -> none  [per_device(): total_sum = lax.psum(local_sum, ('tm', 'space'))]
    reduce_sum x8 -> x0, other arithmetic: 40.4 us -> none  [the longest x7 39 us: restrict(): field.reshape(depth // 4, 4, rows // 4, 4, cols // 4, 4)]
    ppermute x20 -> x0, waiting for transfers between devices: 25.7 us -> none  [the longest x6 17.2 us: padded_2(): after = lax.ppermute(first, axis, down)]
    another operation x1 -> x0, local copies, waits for them, and re-layouts: 14.3 us -> none  [restrict(): field.reshape(depth // 4, 4, rows // 4, 4, cols // 4, 4)]
    all_gather x1 -> x0, blocking collectives: 11.7 us -> none  [per_device(): coarse_set = lax.all_gather(coarse_set, 'space', axis=1, tiled=True)]
  transfers between devices with their start and end apart: 20 -> 0, of which waited for: 16 -> 0; matrix products, arithmetic and copies ran while one was open for 31% -> 0% of each run, Pallas kernels for 0% -> 0%
where the time goes in v1:
time: 54 us; the launch traced here: 53 us
  Pallas kernels  44.9 us (83%)
  local copies, waits for them, and re-layouts  5.72 us (11%)
  between operations  2.34 us (4%)
    pallas_call x1, Pallas kernels, per_device(): pl.pallas_call(functools.partial(kernel, T, S), out_shape=(jax.ShapeDtype...  44.9 us
    unnamed x11, local copies, waits for them, and re-layouts  5.72 us

profile of v1, /device:TPU:0, one launch (start us, length us, event | category | flops | bytes accessed | tf_op | source)
XLA Modules:
  0.0 53.0 jit_solution(18348514700051887397)
XLA Ops:
  0.6 0.0 copy-start
  0.6 1.0 %copy-done = f32[1,12,64,128]{3,2,1,0:T(8,128)S(1)} copy-done((f32[1,12,64,128]{3,2,1,0:T(8,128)S(1)}, f32[1,12,64,128]{3,2,1,0:T(8,128)}, u32[]{:S(2)}) %copy-start) | copy-done | bytes 393240
  1.6 0.0 copy-start.1
  1.6 1.0 %copy-done.1 = f32[12,64,128]{2,1,0:T(8,128)S(1)} copy-done((f32[12,64,128]{2,1,0:T(8,128)S(1)}, f32[12,64,128]{2,1,0:T(8,128)}, u32[]{:S(2)}) %copy-start.1) | copy-done | bytes 393240
  2.6 0.0 copy-start.2
  2.6 1.0 %copy-done.2 = f32[12,64,128]{2,1,0:T(8,128)S(1)} copy-done((f32[12,64,128]{2,1,0:T(8,128)S(1)}, f32[12,64,128]{2,1,0:T(8,128)}, u32[]{:S(2)}) %copy-start.2) | copy-done | bytes 393240
  3.6 0.0 copy-start.3
  3.6 1.0 %copy-done.3 = f32[12,64,128]{2,1,0:T(8,128)S(1)} copy-done((f32[12,64,128]{2,1,0:T(8,128)S(1)}, f32[12,64,128]{2,1,0:T(8,128)}, u32[]{:S(2)}) %copy-start.3) | copy-done | bytes 393240
  4.6 0.0 copy-start.4
  4.6 1.0 %copy-done.4 = f32[12,64,128]{2,1,0:T(8,128)S(1)} copy-done((f32[12,64,128]{2,1,0:T(8,128)S(1)}, f32[12,64,128]{2,1,0:T(8,128)}, u32[]{:S(2)}) %copy-start.4) | copy-done | bytes 393240
  5.6 44.9 %shard_map.68 = (f32[1,12,64,128]{3,2,1,0:T(8,128)S(1)}, f32[1,1]{1,0:T(1,128)}) custom-call(f32[1,12,64,128]{3,2,1,0:T(8,128)S(1)} %copy-done, f32[12,64,128]{2,1,0:T(8,128)S(1)} %copy-done.1, f32[12,64,128]{2,1,0:T(8,128)S(1)} %copy-done.2, f32[12,64,128]{2,1,0:T(8,128)S(1)} %copy-done.3, f32[12,64,128]{2,1,0:T(8,128)S(1)} %copy-done.4), custom_call_target="tpu_custom_call" | custom-call | tf_op jit(solution)/shard_map/pallas_call | solution.py:452
  50.5 0.7 %copy.9 = f32[1,12,64,128]{3,2,1,0:T(8,128)} copy(f32[1,12,64,128]{3,2,1,0:T(8,128)S(1)} %get-tuple-element.8) | data formatting | bytes 786432
Async XLA Ops:
  0.6 1.0 %copy-start = (f32[1,12,64,128]{3,2,1,0:T(8,128)S(1)}, f32[1,12,64,128]{3,2,1,0:T(8,128)}, u32[]{:S(2)}) copy-start(f32[1,12,64,128]{3,2,1,0:T(8,128)} %st_hbm.1) | copy-start | bytes 1179652
  1.6 1.0 %copy-start.1 = (f32[12,64,128]{2,1,0:T(8,128)S(1)}, f32[12,64,128]{2,1,0:T(8,128)}, u32[]{:S(2)}) copy-start(f32[12,64,128]{2,1,0:T(8,128)} %vx_hbm.1) | copy-start | bytes 1179652
  2.6 1.0 %copy-start.2 = (f32[12,64,128]{2,1,0:T(8,128)S(1)}, f32[12,64,128]{2,1,0:T(8,128)}, u32[]{:S(2)}) copy-start(f32[12,64,128]{2,1,0:T(8,128)} %vy_hbm.1) | copy-start | bytes 1179652
  3.6 1.0 %copy-start.3 = (f32[12,64,128]{2,1,0:T(8,128)S(1)}, f32[12,64,128]{2,1,0:T(8,128)}, u32[]{:S(2)}) copy-start(f32[12,64,128]{2,1,0:T(8,128)} %vz_hbm.1) | copy-start | bytes 1179652
  4.6 1.0 %copy-start.4 = (f32[12,64,128]{2,1,0:T(8,128)S(1)}, f32[12,64,128]{2,1,0:T(8,128)}, u32[]{:S(2)}) copy-start(f32[12,64,128]{2,1,0:T(8,128)} %kp_hbm.1) | copy-start | bytes 1179652

commit v2 on v1

--- a/solution.py
+++ b/solution.py
@@ -12,6 +12,7 @@
 B = 4
 ROUNDS = (2, 2, 2)
 HALO = max(ROUNDS)
+STEP_PLANES = (14, 12, 7, 4, 2, 1)
 MESH = pl.DeviceIdType.MESH
 
 
@@ -72,24 +73,20 @@
     T, S,
     st_hbm, vx_hbm, vy_hbm, vz_hbm, kp_hbm,
     out_ref, chg_ref,
-    cx, co, U, V, st, F, wloc, wg, ccloc, ccg, qloc, qg, full, cfull, cw, hs,
+    cx, co, U, V, st, F, wloc, wg, ccloc, ccg, qloc, qg, qsum, qsums, full, cfull, cw, hs,
     lsem, usend, urecv, csend, crecv, hsend, hrecv, ccsend, ccrecv,
-    wsend, wrecv, qsend, qrecv,
+    wsend, wrecv, qsend, qrecv, ysend, yrecv, ready,
 ):
     depth, Y, X = st.shape
     N = T * S
     t = lax.axis_index("tm")
     s = lax.axis_index("space")
-    me = t * S + s
     planes = depth // B
     slab_rows = planes * Y // B**2
     plane_rows = Y // B**2
     pad_rows = wloc.shape[0]
     H = HALO
     coefs = (vx_hbm, vy_hbm, vz_hbm, kp_hbm)
-
-    def peer(i):
-        return lax.rem(t + i // S, T), lax.rem(s + lax.rem(i, S), S)
 
     loads = [
         pltpu.make_async_copy(c, cx.at[i, pl.ds(H - 1, depth)], lsem.at[i])
@@ -102,11 +99,30 @@
 
     barrier = pltpu.get_barrier_semaphore()
 
-    def greet(i, _):
-        pl.semaphore_signal(barrier, inc=1, device_id=peer(i), device_id_type=MESH)
-        return 0
-
-    lax.fori_loop(1, N, greet, 0)
+    up_t = lax.rem(t + 1, T)
+    down_t = lax.rem(t + T - 1, T)
+    up_s = lax.rem(s + 1, S)
+    down_s = lax.rem(s + S - 1, S)
+    has_up = s < S - 1
+    has_down = s > 0
+    moves = t < T - 1
+    works = t > 0
+
+    def greet(device):
+        pl.semaphore_signal(barrier, inc=1, device_id=device, device_id_type=MESH)
+
+    @pl.when(works & has_up)
+    def _():
+        greet((down_t, up_s))
+
+    @pl.when(works & has_down)
+    def _():
+        greet((down_t, down_s))
+
+    for j in range(1, T):
+        greet((lax.rem(t + j, T), s))
+    for j in range(1, S):
+        greet((t, lax.rem(s + j, S)))
 
     @pl.when(s == 0)
     def _():
@@ -145,7 +161,13 @@
         ccloc[i] = pool(jnp.concatenate(sums, axis=0), pad_rows)
     ccg[pl.ds(s, 1)] = ccloc[...][None]
 
-    pl.semaphore_wait(barrier, N - 1)
+    across = jnp.where(has_up, 1, 0) + jnp.where(has_down, 1, 0)
+    pl.semaphore_wait(barrier, T + S - 2 + jnp.where(moves, across, 0))
+
+    for j in range(1, S):
+        pl.semaphore_signal(
+            ready, inc=1, device_id=(t, lax.rem(s + j, S)), device_id_type=MESH
+        )
 
     def remote(src, dst, send, recv, device):
         return pltpu.make_async_remote_copy(
@@ -154,13 +176,6 @@
         )
 
     d0 = ROUNDS[0]
-    up_t = lax.rem(t + 1, T)
-    up_s = lax.rem(s + 1, S)
-    down_s = lax.rem(s + S - 1, S)
-    has_up = s < S - 1
-    has_down = s > 0
-    moves = t < T - 1
-    works = t > 0
     low0 = remote(st_hbm.at[0, pl.ds(depth - d0, d0)], U.at[0, pl.ds(H - d0, d0)],
                   usend.at[0], urecv.at[0], (up_t, up_s))
     high0 = remote(st_hbm.at[0, pl.ds(0, d0)], U.at[0, pl.ds(H + depth, d0)],
@@ -208,26 +223,37 @@
         cc_copy(j, s).start()
 
     def step(src, dst, lo, hi):
-        def body(z, _):
-            u = src[z]
-            v = co[0, z - 1] * u
-            v += co[1, z - 1] * pltpu.roll(u, 1, 1)
-            v += co[2, z - 1] * pltpu.roll(u, X - 1, 1)
-            v += co[3, z - 1] * pltpu.roll(u, 1, 0)
-            v += co[4, z - 1] * pltpu.roll(u, Y - 1, 0)
-            v += co[5, z - 1] * src[z - 1]
-            v += co[6, z - 1] * src[z + 1]
-            dst[z] = v
+        group = next(g for g in STEP_PLANES if (hi - lo) % g == 0)
+
+        def body(i, _):
+            z = lo + i * group
+            u = [src[z - 1 + k] for k in range(group + 2)]
+            new = []
+            for k in range(group):
+                c, n = u[k + 1], z - 1 + k
+                v = co[0, n] * c + co[5, n] * u[k] + co[6, n] * u[k + 2]
+                v += co[3, n] * pltpu.roll(c, 1, 0) + co[4, n] * pltpu.roll(c, Y - 1, 0)
+                v += co[1, n] * pltpu.roll(c, 1, 1) + co[2, n] * pltpu.roll(c, X - 1, 1)
+                new.append(v)
+            for k in range(group):
+                dst[z + k] = new[k]
             return 0
 
-        lax.fori_loop(lo, hi, body, 0)
-
-    def w_copy(i, slot):
-        return remote(wloc.at[pl.ds(0, slab_rows)], wg.at[slot, pl.ds(0, slab_rows)],
-                      wsend.at[i], wrecv.at[slot], peer(i))
-
-    def q_copy(i, slot):
-        return remote(qloc, qg.at[slot], qsend.at[i], qrecv.at[slot], peer(i))
+        lax.fori_loop(0, (hi - lo) // group, body, 0)
+
+    def w_copy(j, k, slice_from, place):
+        return remote(wloc.at[pl.ds(0, slab_rows)],
+                      wg.at[place, slice_from, pl.ds(0, slab_rows)],
+                      wsend.at[j, k], wrecv.at[place, slice_from],
+                      (lax.rem(t + j, T), lax.rem(s + k, S)))
+
+    def q_copy(j, slice_from):
+        return remote(qloc, qg.at[slice_from], qsend.at[j], qrecv.at[slice_from],
+                      (lax.rem(t + j, T), s))
+
+    def sum_copy(j, place):
+        return remote(qsum, qsums.at[place], ysend.at[j], yrecv.at[place],
+                      (t, lax.rem(s + j, S)))
 
     @pl.when(works)
     def _():
@@ -301,13 +327,13 @@
                 total = f if total is None else total + f
             sums.append(total)
         wloc[...] = pool(jnp.concatenate(sums, axis=0), pad_rows)
-
-        def send_w(i, _):
-            w_copy(i, me).start()
-            return 0
-
-        lax.fori_loop(1, N, send_w, 0)
-        wg[pl.ds(me, 1)] = wloc[...][None]
+        pl.semaphore_wait(ready, S - 1)
+
+        for j in range(T):
+            for k in range(S):
+                if j or k:
+                    w_copy(j, k, t, s).start()
+        wg[pl.ds(s, 1), pl.ds(t, 1)] = wloc[...][None, None]
 
         wide = prolong(wloc[...], planes * Y, 0)
         q = jnp.zeros((8, X), jnp.float32)
@@ -318,12 +344,13 @@
                 q += jnp.sum((g * g).reshape(Y // 8, 8, X), axis=0)
         qloc[...] = jnp.sum(q, axis=0, keepdims=True)
 
-        def send_q(i, _):
-            q_copy(i, me).start()
-            return 0
-
-        lax.fori_loop(1, N, send_q, 0)
-        qg[pl.ds(me, 1)] = qloc[...][None]
+        for j in range(1, T):
+            q_copy(j, t).start()
+        qg[pl.ds(t, 1)] = qloc[...][None]
+
+    @pl.when(t == 0)
+    def _():
+        pl.semaphore_wait(ready, S - 1)
 
     for j in range(1, S):
         cc_copy(j, lax.rem(s + S - j, S)).wait_recv()
@@ -364,17 +391,27 @@
             u = v
         return u
 
-    def arrival(copy, slot):
-        @pl.when(slot != me)
-        def _():
-            copy(1, slot).wait_recv()
+    total = jnp.zeros((1, X), jnp.float32)
+    for m in range(1, T):
+
+        @pl.when(t != m)
+        def _(m=m):
+            q_copy(1, m).wait_recv()
+
+        total = total + qg[m]
+    qsum[...] = total
+    for j in range(1, S):
+        sum_copy(j, s).start()
 
     def chain(m, carry):
         jump, squares = carry
         for p in range(S):
-            arrival(w_copy, m * S + p)
+            @pl.when((t != m) | (s != p))
+            def _(p=p):
+                w_copy(1, 0, m, p).wait_recv()
+
         for p in range(S):
-            full[p * slab_rows : (p + 1) * slab_rows] = wg[m * S + p, 0:slab_rows]
+            full[p * slab_rows : (p + 1) * slab_rows] = wg[p, m, 0:slab_rows]
         moved = coarse(jump)
         hs[m] = moved
         jump = full[...] + moved
@@ -394,11 +431,10 @@
     def _():
         out_ref[0] = st[...]
 
-    def gather_q(i, total):
-        arrival(q_copy, i)
-        return total + qg[i]
-
-    total = lax.fori_loop(S, N, gather_q, jnp.zeros((1, X), jnp.float32))
+    for j in range(1, S):
+        place = lax.rem(s + S - j, S)
+        sum_copy(j, place).wait_recv()
+        total = total + qsums[place]
     total = total + float(B**3) * jnp.sum(squares, axis=0, keepdims=True)
     total = jnp.sum(total, axis=1, keepdims=True)
     count = N * depth * Y * X
@@ -406,6 +442,7 @@
 
     for j in range(1, S):
         cc_copy(j, s).wait_send()
+        sum_copy(j, s).wait_send()
 
     @pl.when(moves)
     def _():
@@ -431,12 +468,12 @@
 
     @pl.when(works)
     def _():
-        def done(i, _):
-            w_copy(i, me).wait_send()
-            q_copy(i, me).wait_send()
-            return 0
-
-        lax.fori_loop(1, N, done, 0)
+        for j in range(1, T):
+            q_copy(j, t).wait_send()
+        for j in range(T):
+            for k in range(S):
+                if j or k:
+                    w_copy(j, k, t, s).wait_send()
 
 
 def per_device(T, S, starts, vel_x, vel_y, vel_z, kappa):
@@ -444,7 +481,6 @@
     slab_rows = depth // B * Y // B**2
     pad_rows = -(-slab_rows // 8) * 8
     rows = S * slab_rows
-    N = T * S
     R = len(ROUNDS)
     vmem = lambda *shape: pltpu.VMEM(shape, jnp.float32)
     dma = lambda *shape: pltpu.SemaphoreType.DMA(shape)
@@ -468,11 +504,13 @@
             vmem(depth, Y, X),
             vmem(depth, Y, X),
             vmem(pad_rows, X),
-            vmem(N, pad_rows, X),
+            vmem(S, T, pad_rows, X),
             vmem(4, pad_rows, X),
             vmem(S, 4, pad_rows, X),
             vmem(1, X),
-            vmem(N, 1, X),
+            vmem(T, 1, X),
+            vmem(1, X),
+            vmem(S, 1, X),
             vmem(rows, X),
             vmem(4, rows, X),
             vmem(7, rows, X),
@@ -482,11 +520,13 @@
             dma(2, 4), dma(2, 4),
             dma(R, 2), dma(R, 2),
             dma(S), dma(S),
-            dma(N), dma(N),
-            dma(N), dma(N),
+            dma(T, S), dma(S, T),
+            dma(T), dma(T),
+            dma(S), dma(S),
+            pltpu.SemaphoreType.REGULAR,
         ],
         compiler_params=pltpu.CompilerParams(
-            collective_id=0, has_side_effects=True, vmem_limit_bytes=40 * 2**20
+            collective_id=0, has_side_effects=True, vmem_limit_bytes=60 * 2**20
         ),
     )(starts, vel_x, vel_y, vel_z, kappa)
     return new, change[0, 0]

time: 54 us -> 44.4 us (0.82); the launches traced: 53 us -> 44.2 us
  Pallas kernels: 44.9 us -> 40 us
  local copies, waits for them, and re-layouts: 5.72 us -> 1.77 us
    pallas_call x1, Pallas kernels: 44.9 us -> 40 us  [per_device(): pl.pallas_call(functools.partial(kernel, T, S), out_shape=(jax.ShapeDtype...]
    unnamed x11 -> x1, local copies, waits for them, and re-layouts: 5.72 us -> 1.77 us
where the time goes in v2:
time: 44.4 us; the launch traced here: 44.2 us
  Pallas kernels  40 us (90%)
  between operations  2.39 us (5%)
  local copies, waits for them, and re-layouts  1.77 us (4%)
    pallas_call x1, Pallas kernels, per_device(): pl.pallas_call(functools.partial(kernel, T, S), out_shape=(jax.ShapeDtype...  40 us
    unnamed x1, local copies, waits for them, and re-layouts  1.77 us

profile of v2, /device:TPU:0, one launch (start us, length us, event | category | flops | bytes accessed | tf_op | source)
XLA Modules:
  0.0 44.2 jit_solution(11937400358843781246)
XLA Ops:
  0.6 40.0 %shard_map.68 = (f32[1,12,64,128]{3,2,1,0:T(8,128)}, f32[1,1]{1,0:T(1,128)}) custom-call(f32[1,12,64,128]{3,2,1,0:T(8,128)} %st_hbm.1, f32[12,64,128]{2,1,0:T(8,128)} %vx_hbm.1, f32[12,64,128]{2,1,0:T(8,128)} %vy_hbm.1, f32[12,64,128]{2,1,0:T(8,128)} %vz_hbm.1, f32[12,64,128]{2,1,0:T(8,128)} %kp_hbm.1), custom_call_target="tpu_custom_call" | custom-call | tf_op jit(solution)/shard_map/pallas_call | solution.py:488
  40.7 1.8 %copy.9 = f32[1,12,64,128]{3,2,1,0:T(8,128)} copy(f32[1,12,64,128]{3,2,1,0:T(8,128)} %get-tuple-element.8) | data formatting | bytes 786432

commit v3 on v2

--- a/solution.py
+++ b/solution.py
@@ -10,9 +10,9 @@
 FSTEPS = 6
 GC = 2
 B = 4
-ROUNDS = (2, 2, 2)
+ROUNDS = (3, 3)
 HALO = max(ROUNDS)
-STEP_PLANES = (14, 12, 7, 4, 2, 1)
+STEP_PLANES = (16, 14, 12, 7, 4, 2, 1)
 MESH = pl.DeviceIdType.MESH
 
 
@@ -75,7 +75,7 @@
     out_ref, chg_ref,
     cx, co, U, V, st, F, wloc, wg, ccloc, ccg, qloc, qg, qsum, qsums, full, cfull, cw, hs,
     lsem, usend, urecv, csend, crecv, hsend, hrecv, ccsend, ccrecv,
-    wsend, wrecv, qsend, qrecv, ysend, yrecv, ready,
+    wsend, wrecv, qsend, qrecv, ysend, yrecv, ready, fsend, frecv,
 ):
     depth, Y, X = st.shape
     N = T * S
@@ -193,27 +193,48 @@
         for i, c in enumerate(coefs)
     ] if H > 1 else []
 
+    half = lax.rem(t, 2)
+    pair = t + 1 - 2 * half
+    low_f = [
+        remote(cx.at[i, pl.ds(0, H - 1)], cx.at[i, pl.ds(0, H - 1)],
+               fsend.at[0, i], frecv.at[0, i], (pair, s))
+        for i in range(4)
+    ]
+    high_f = [
+        remote(cx.at[i, pl.ds(H - 1 + depth, H - 1)], cx.at[i, pl.ds(H - 1 + depth, H - 1)],
+               fsend.at[1, i], frecv.at[1, i], (pair, s))
+        for i in range(4)
+    ]
+
+    def for_mine(cond, *acts):
+        for h in range(2):
+            @pl.when((half == h) & cond)
+            def _(h=h):
+                for i in (2 * h, 2 * h + 1):
+                    for act in acts:
+                        act(i)
+
+    def for_others(cond, act):
+        for h in range(2):
+            @pl.when((half != h) & cond)
+            def _(h=h):
+                for i in (2 * h, 2 * h + 1):
+                    act(i)
+
+    for_mine(has_up, lambda i: low_c[i].start())
+    for_mine(has_down, lambda i: high_c[i].start())
+
+    @pl.when(moves & has_up)
+    def _():
+        low0.start()
+
+    @pl.when(moves & has_down)
+    def _():
+        high0.start()
+
     @pl.when(moves)
     def _():
         main0.start()
-
-    @pl.when(moves & has_up)
-    def _():
-        low0.start()
-
-    @pl.when(moves & has_down)
-    def _():
-        high0.start()
-
-    @pl.when(works & has_up)
-    def _():
-        for c in low_c:
-            c.start()
-
-    @pl.when(works & has_down)
-    def _():
-        for c in high_c:
-            c.start()
 
     def cc_copy(j, slot):
         return remote(ccloc, ccg.at[slot], ccsend.at[j], ccrecv.at[slot],
@@ -255,29 +276,23 @@
         return remote(qsum, qsums.at[place], ysend.at[j], yrecv.at[place],
                       (t, lax.rem(s + j, S)))
 
+    for_mine(has_down, lambda i: low_c[i].wait_recv(), lambda i: low_f[i].start())
+    for_mine(has_up, lambda i: high_c[i].wait_recv(), lambda i: high_f[i].start())
+    for_others(has_down, lambda i: low_f[i].wait_recv())
+    for_others(has_up, lambda i: high_f[i].wait_recv())
+
     @pl.when(works)
     def _():
+        lax.fori_loop(0, H - 1, fill, 0)
+        lax.fori_loop(H - 1 + depth, 2 * H - 2 + depth, fill, 0)
+
         @pl.when(has_down)
         def _():
-            for c in low_c:
-                c.wait_recv()
-            lax.fori_loop(0, H - 1, fill, 0)
             low0.wait_recv()
 
         @pl.when(has_up)
         def _():
-            for c in high_c:
-                c.wait_recv()
-            lax.fori_loop(H - 1 + depth, 2 * H - 2 + depth, fill, 0)
             high0.wait_recv()
-
-        @pl.when(s == 0)
-        def _():
-            lax.fori_loop(0, H - 1, fill, 0)
-
-        @pl.when(s == S - 1)
-        def _():
-            lax.fori_loop(H - 1 + depth, 2 * H - 2 + depth, fill, 0)
 
         main0.wait_recv()
 
@@ -456,15 +471,8 @@
     def _():
         high0.wait_send()
 
-    @pl.when(works & has_up)
-    def _():
-        for c in low_c:
-            c.wait_send()
-
-    @pl.when(works & has_down)
-    def _():
-        for c in high_c:
-            c.wait_send()
+    for_mine(has_up, lambda i: low_c[i].wait_send(), lambda i: high_f[i].wait_send())
+    for_mine(has_down, lambda i: high_c[i].wait_send(), lambda i: low_f[i].wait_send())
 
     @pl.when(works)
     def _():
@@ -524,6 +532,7 @@
             dma(T), dma(T),
             dma(S), dma(S),
             pltpu.SemaphoreType.REGULAR,
+            dma(2, 4), dma(2, 4),
         ],
         compiler_params=pltpu.CompilerParams(
             collective_id=0, has_side_effects=True, vmem_limit_bytes=60 * 2**20

time: 44.4 us -> 40.3 us (0.908)
  Pallas kernels: 40 us -> 35.9 us
    pallas_call x1, Pallas kernels: 40 us -> 35.9 us  [per_device(): pl.pallas_call(functools.partial(kernel, T, S), out_shape=(jax.ShapeDtype...]
where the time goes in v3:
time: 40.3 us; the launch traced here: 40 us
  Pallas kernels  35.9 us (89%)
  between operations  2.39 us (6%)
  local copies, waits for them, and re-layouts  1.77 us (4%)
    pallas_call x1, Pallas kernels, per_device(): pl.pallas_call(functools.partial(kernel, T, S), out_shape=(jax.ShapeDtype...  35.9 us
    unnamed x1, local copies, waits for them, and re-layouts  1.77 us

profile of v3, /device:TPU:0, one launch (start us, length us, event | category | flops | bytes accessed | tf_op | source)
XLA Modules:
  0.0 40.0 jit_solution(9673220198155963329)
XLA Ops:
  0.6 35.9 %shard_map.68 = (f32[1,12,64,128]{3,2,1,0:T(8,128)}, f32[1,1]{1,0:T(1,128)}) custom-call(f32[1,12,64,128]{3,2,1,0:T(8,128)} %st_hbm.1, f32[12,64,128]{2,1,0:T(8,128)} %vx_hbm.1, f32[12,64,128]{2,1,0:T(8,128)} %vy_hbm.1, f32[12,64,128]{2,1,0:T(8,128)} %vz_hbm.1, f32[12,64,128]{2,1,0:T(8,128)} %kp_hbm.1), custom_call_target="tpu_custom_call" | custom-call | tf_op jit(solution)/shard_map/pallas_call | solution.py:496
  36.5 1.8 %copy.9 = f32[1,12,64,128]{3,2,1,0:T(8,128)} copy(f32[1,12,64,128]{3,2,1,0:T(8,128)} %get-tuple-element.8) | data formatting | bytes 786432
